TPU v7x, 32 devices: a whole 2x2x4 slice. The times are simulated.
32 devices in a mesh: seg: 4 (over y, core), band: 8 (over z, x).
Axes of the slice: x: 2, y: 2, z: 4, core: 2. Of those that a mesh axis runs over, the one named last changes fastest.
Arguments:
- sft: bfloat16 [8, 2, 2, 2048], P('seg', None, None, 'band'), may hold values from -6 to 6
- doppler: float32 [8, 512], P('seg'), may hold values from -16 to 16
- antenna: float32 [8, 2, 2, 512], P('seg'), may hold values from -1 to 1
- coarse_index: int32 [8, 128], P('seg'), may hold values from 0 to 511
- freq_offset: int32 [8, 128], P('seg'), may hold values from -32 to 32
- wing_width: int32 [8], replicated, may hold values from 8 to 32
Outputs:
- fstat: float32 [128, 2048], P('seg', 'band')
All inputs are finite; a program needn't handle non-finite values.
Results may differ from a plain program's by a relative error of at most 0.00088.
Values may be sent and summed in bfloat16 or wider, within the bound.
A program may use at most 64 MiB of HBM per device.

v0:
```python
import functools
import math

import jax
import jax.numpy as jnp
from jax import lax
from jax.experimental import pallas as pl
from jax.experimental.pallas import tpu as pltpu
from jax.sharding import PartitionSpec as P

WMAX = 32
OMAX = 32
TAPS = 2 * WMAX
LANES = 128
ROWS = 8
MESH = pl.DeviceIdType.MESH


def half_turn(x):
    rest = x - jnp.round(x)
    angle = rest * math.pi
    square = angle * angle
    sine = jnp.zeros_like(x)
    cosine = jnp.zeros_like(x)
    for power in range(7, -1, -1):
        sign = -1.0 if power % 2 else 1.0
        cosine = cosine * square + sign / math.factorial(2 * power)
        sine = sine * square + sign / math.factorial(2 * power + 1)
    return sine * angle, cosine


def gathered_rows(rows, indices):
    first = rows.astype(jnp.bfloat16).astype(jnp.float32)
    rest = rows - first
    second = rest.astype(jnp.bfloat16).astype(jnp.float32)
    third = rest - second
    parts = jnp.concatenate([first, second, third, jnp.zeros_like(first)], axis=0)
    places = lax.broadcasted_iota(jnp.int32, (rows.shape[1], indices.shape[1]), 0)
    chosen = jnp.where(places == indices, 1.0, 0.0).astype(jnp.bfloat16)
    picked = jnp.dot(parts.astype(jnp.bfloat16), chosen, preferred_element_type=jnp.float32)
    count = rows.shape[0]
    return picked[:count] + picked[count : 2 * count] + picked[2 * count : 3 * count]


def kernel(
    n_seg,
    n_band,
    scale,
    sft_hbm,
    doppler_hbm,
    antenna_hbm,
    index_hbm,
    offset_hbm,
    wing_hbm,
    out_ref,
    sft_ref,
    doppler_ref,
    antenna_ref,
    index_ref,
    offset_ref,
    wing_ref,
    x_ref,
    edge_ref,
    param_ref,
    fine_ref,
    column_ref,
    kernel_ref,
    part_ref,
    recv_ref,
    load_sem,
    edge_send,
    edge_recv,
    part_send,
    part_recv,
):
    seg = lax.axis_index("seg")
    band = lax.axis_index("band")
    segs_here, dets, _, bins = sft_ref.shape
    fine = index_ref.shape[1]
    own = fine // n_seg
    lines = 2 * dets
    has_up = band < n_band - 1
    has_down = band > 0
    up = jnp.minimum(band + 1, n_band - 1)
    down = jnp.maximum(band - 1, 0)

    barrier = pltpu.get_barrier_semaphore()
    for there, neighbour in ((has_up, up), (has_down, down)):

        @pl.when(there)
        def _():
            pl.semaphore_signal(
                barrier, inc=1, device_id={"band": neighbour}, device_id_type=MESH
            )

    for step in range(1, n_seg):
        pl.semaphore_signal(
            barrier,
            inc=1,
            device_id={"seg": lax.rem(seg + step, n_seg)},
            device_id_type=MESH,
        )

    loads = []
    for source, target in (
        (sft_hbm, sft_ref),
        (doppler_hbm, doppler_ref),
        (antenna_hbm, antenna_ref),
        (index_hbm, index_ref),
        (offset_hbm, offset_ref),
        (wing_hbm, wing_ref),
    ):
        loads.append(pltpu.make_async_copy(source, target, load_sem.at[len(loads)]))
        loads[-1].start()
    loads[0].wait()
    for s in range(segs_here):
        for d in range(dets):
            first = s * lines + 2 * d
            x_ref[first : first + 2, :] = sft_ref[s, d].astype(jnp.float32)
    neighbours = n_seg - 1 + has_up.astype(jnp.int32) + has_down.astype(jnp.int32)
    pl.semaphore_wait(barrier, neighbours)

    def edge_copy(side):
        start, neighbour = ((bins - LANES, up), (0, down))[side]
        return pltpu.make_async_remote_copy(
            src_ref=x_ref.at[:, pl.ds(start, LANES)],
            dst_ref=edge_ref.at[side],
            send_sem=edge_send.at[side],
            recv_sem=edge_recv.at[side],
            device_id={"band": neighbour},
            device_id_type=MESH,
        )

    for side, there in enumerate((has_up, has_down)):

        @pl.when(there)
        def _():
            edge_copy(side).start()

    for load in loads[1:]:
        load.wait()
    param_ref[...] = jnp.zeros_like(param_ref)
    fine_ref[...] = jnp.zeros_like(fine_ref)
    for s in range(segs_here):
        param_ref[ROWS * s : ROWS * s + 1, :] = doppler_ref[s : s + 1, :]
        for q in range(2):
            first = ROWS * s + 1 + dets * q
            param_ref[first : first + dets, :] = antenna_ref[s, q]
    for s in range(segs_here):
        rows = gathered_rows(param_ref[ROWS * s : ROWS * (s + 1), :], index_ref[s : s + 1, :])
        fine_ref[ROWS * s : ROWS * (s + 1), :] = rows
        sine, cosine = half_turn(rows[0:1])
        fine_ref[ROWS * s + 5 : ROWS * s + 6, :] = offset_ref[s : s + 1, :].astype(jnp.float32)
        fine_ref[ROWS * s + 6 : ROWS * s + 7, :] = sine
        fine_ref[ROWS * s + 7 : ROWS * s + 8, :] = cosine
    columns = jnp.transpose(fine_ref[...])
    column_ref[...] = columns

    lane = lax.broadcasted_iota(jnp.int32, (fine, 2 * TAPS), 1)
    from_real = lane < TAPS
    tap = (WMAX - 1 - lax.rem(lane, TAPS)).astype(jnp.float32)
    for s in range(segs_here):
        column = lambda row: columns[:, ROWS * s + row : ROWS * s + row + 1]
        u = tap - column(0)
        centre = u == 0.0
        envelope = jnp.where(
            centre, 1.0, -column(6) / jnp.where(centre, 1.0, math.pi * u)
        )
        real_part = envelope * column(7)
        imag_part = envelope * column(6)
        to_real = jnp.where(from_real, real_part, -imag_part)
        to_imag = jnp.where(from_real, imag_part, real_part)
        for q in range(2):
            for part, shape in enumerate((to_real, to_imag)):
                for d in range(dets):
                    piece = column(1 + dets * q + d) * shape
                    kernel_ref[s, 2 * q + part, :, 2 * TAPS * d : 2 * TAPS * (d + 1)] = (
                        piece.astype(jnp.bfloat16)
                    )

    width = bins + 2 * (WMAX + OMAX)
    wing_low = jnp.where(has_down, wing_ref[down], 0)
    wing_mid = wing_ref[band]
    wing_high = jnp.where(has_up, wing_ref[up], 0)
    position = lax.broadcasted_iota(jnp.int32, (TAPS, width), 1)
    reach = jnp.where(
        position < OMAX, wing_low, jnp.where(position < OMAX + bins, wing_mid, wing_high)
    )
    tap_here = WMAX - 1 - lax.broadcasted_iota(jnp.int32, (TAPS, width), 0)
    inside = (tap_here >= -reach) & (tap_here < reach)

    for side, there in enumerate((has_down, has_up)):

        @pl.when(there)
        def _():
            edge_copy(side).wait_recv()

    low = jnp.where(has_down, edge_ref[0], 0.0)
    high = jnp.where(has_up, edge_ref[1], 0.0)
    padded = jnp.concatenate([low, x_ref[...], high], axis=1)
    margin = LANES - WMAX - OMAX
    padded = pltpu.roll(padded, padded.shape[1] - margin, 1)[:, :width]

    transforms = []
    for s in range(segs_here):
        unfolded = []
        for line in range(s * lines, (s + 1) * lines):
            spread = jnp.broadcast_to(padded[line : line + 1, :], (TAPS, width))
            spread = pltpu.roll(spread, width - TAPS + 1, 1, stride=1, stride_axis=0)
            unfolded.append(jnp.where(inside, spread, 0.0))
        transforms.append(jnp.concatenate(unfolded, axis=0).astype(jnp.bfloat16))

    def fine_block(owner):
        rows = pl.ds(pl.multiple_of(owner * own, own), own)
        columns = column_ref[rows, :]
        total = None
        for s in range(segs_here):
            taps = jnp.concatenate([kernel_ref[s, part, rows, :] for part in range(4)], axis=0)
            amplitude = jnp.dot(taps, transforms[s], preferred_element_type=jnp.float32)
            power = amplitude * amplitude
            coarse = (power[:own] + power[own : 2 * own]) + (
                power[2 * own : 3 * own] + power[3 * own :]
            )
            shift = columns[:, ROWS * s + 5 : ROWS * s + 6].astype(jnp.int32) + OMAX
            for bit in range((2 * OMAX).bit_length()):
                moved = pltpu.roll(coarse, width - (1 << bit), 1)
                coarse = jnp.where((shift & (1 << bit)) != 0, moved, coarse)
            total = coarse[:, :bins] if total is None else total + coarse[:, :bins]
        return total * scale

    sends = []
    for step in range(1, n_seg):
        peer = lax.rem(seg + step, n_seg)
        part_ref[step - 1] = fine_block(peer)
        sends.append(
            pltpu.make_async_remote_copy(
                src_ref=part_ref.at[step - 1],
                dst_ref=recv_ref.at[step - 1],
                send_sem=part_send.at[step - 1],
                recv_sem=part_recv.at[step - 1],
                device_id={"seg": peer},
                device_id_type=MESH,
            )
        )
        sends[-1].start()
    result = fine_block(seg)
    for step in range(1, n_seg):
        sends[step - 1].wait_recv()
        result = result + recv_ref[step - 1]
    out_ref[...] = result
    for send in sends:
        send.wait_send()
    for side, there in enumerate((has_up, has_down)):

        @pl.when(there)
        def _():
            edge_copy(side).wait_send()


def solution(mesh):
    n_seg = mesh.shape["seg"]
    n_band = mesh.shape["band"]
    placed = (
        P("seg", None, None, "band"),
        P("seg", None),
        P("seg", None, None, None),
        P("seg", None),
        P("seg", None),
        P(),
    )

    def per_device(sft, doppler, antenna, coarse_index, freq_offset, wing_width):
        segs_here, dets, _, bins = sft.shape
        fine = coarse_index.shape[1]
        own = fine // n_seg
        lines = segs_here * dets * 2
        operands = [
            pltpu.with_memory_space_constraint(operand, pltpu.HBM)
            for operand in (sft, doppler, antenna, coarse_index, freq_offset, wing_width)
        ]
        vmem = pl.BlockSpec(memory_space=pltpu.VMEM)
        hbm = pl.BlockSpec(memory_space=pltpu.HBM)
        return pl.pallas_call(
            functools.partial(kernel, n_seg, n_band, 0.25 / (segs_here * n_seg)),
            out_shape=jax.ShapeDtypeStruct((own, bins), jnp.float32),
            in_specs=[hbm] * 6,
            out_specs=vmem,
            scratch_shapes=[
                pltpu.VMEM(sft.shape, sft.dtype),
                pltpu.VMEM(doppler.shape, doppler.dtype),
                pltpu.VMEM(antenna.shape, antenna.dtype),
                pltpu.VMEM(coarse_index.shape, coarse_index.dtype),
                pltpu.VMEM(freq_offset.shape, freq_offset.dtype),
                pltpu.SMEM(wing_width.shape, wing_width.dtype),
                pltpu.VMEM((lines, bins), jnp.float32),
                pltpu.VMEM((2, lines, LANES), jnp.float32),
                pltpu.VMEM((ROWS * segs_here, doppler.shape[1]), jnp.float32),
                pltpu.VMEM((LANES, fine), jnp.float32),
                pltpu.VMEM((fine, LANES), jnp.float32),
                pltpu.VMEM((segs_here, 4, fine, 2 * TAPS * dets), jnp.bfloat16),
                pltpu.VMEM((n_seg - 1, own, bins), jnp.float32),
                pltpu.VMEM((n_seg - 1, own, bins), jnp.float32),
                pltpu.SemaphoreType.DMA((6,)),
                pltpu.SemaphoreType.DMA((2,)),
                pltpu.SemaphoreType.DMA((2,)),
                pltpu.SemaphoreType.DMA((n_seg - 1,)),
                pltpu.SemaphoreType.DMA((n_seg - 1,)),
            ],
            compiler_params=pltpu.CompilerParams(
                collective_id=0, has_side_effects=True, vmem_limit_bytes=40 * 1024 * 1024
            ),
        )(*operands)

    return jax.shard_map(
        per_device, mesh=mesh, in_specs=placed, out_specs=P("seg", "band"), check_vma=False
    )
```

profile of v0, /device:TPU:1, one launch (start us, length us, event | category | flops | bytes accessed | tf_op | source)
XLA Modules:
  0.0 12.0 jit_solution(5171434723642178886)
XLA Ops:
  0.0 11.4 %shard_map.64 = f32[32,256]{1,0:T(8,128)S(1)} custom-call(bf16[2,2,2,256]{3,2,1,0:T(2,128)(2,1)} %sft_hbm.1, f32[2,512]{1,0:T(2,128)} %doppler_hbm.1, f32[2,2,2,512]{3,2,1,0:T(2,128)} %antenna_hbm.1, s32[2,128]{1,0:T(2,128)} %index_hbm.1, s32[2,128]{1,0:T(2,128)} %offset_hbm.1, s32[8]{0:T(128)} %wing_hbm.1), custom_call_target="tpu_custom_call" | custom-call | tf_op jit(solution)/shard_map/pallas_call | solution.py:283
  11.4 0.6 %copy.8 = f32[32,256]{1,0:T(8,128)} copy(f32[32,256]{1,0:T(8,128)S(1)} %shard_map.64) | data formatting | bytes 65536
where the time goes:
time: 12.2 us; the launch traced here: 12 us
  Pallas kernels  11.4 us (93%)
  local copies, waits for them, and re-layouts  0.62 us (5%)
    pallas_call x1, Pallas kernels, per_device(): pl.pallas_call(functools.partial(kernel, n_seg, n_band, 0.25 / (segs_here...  11.4 us
    unnamed x1, local copies, waits for them, and re-layouts  0.62 us

commit v1 on v0

v1 whole, which is shorter than its diff:
```python
import functools
import math

import jax
import jax.numpy as jnp
from jax import lax
from jax.experimental import pallas as pl
from jax.experimental.pallas import tpu as pltpu
from jax.sharding import PartitionSpec as P

WMAX = 32
OMAX = 32
TAPS = 2 * WMAX
LANES = 128
ROWS = 8
MESH = pl.DeviceIdType.MESH


def half_turn(x):
    rest = x - jnp.round(x)
    angle = rest * math.pi
    square = angle * angle
    sine = jnp.zeros_like(x)
    cosine = jnp.zeros_like(x)
    for power in range(7, -1, -1):
        sign = -1.0 if power % 2 else 1.0
        cosine = cosine * square + sign / math.factorial(2 * power)
        sine = sine * square + sign / math.factorial(2 * power + 1)
    return sine * angle, cosine


def gathered_rows(rows, indices):
    first = rows.astype(jnp.bfloat16).astype(jnp.float32)
    rest = rows - first
    second = rest.astype(jnp.bfloat16).astype(jnp.float32)
    third = rest - second
    parts = jnp.concatenate([first, second, third, jnp.zeros_like(first)], axis=0)
    places = lax.broadcasted_iota(jnp.int32, (rows.shape[1], indices.shape[1]), 0)
    chosen = jnp.where(places == indices, 1.0, 0.0).astype(jnp.bfloat16)
    picked = jnp.dot(parts.astype(jnp.bfloat16), chosen, preferred_element_type=jnp.float32)
    count = rows.shape[0]
    return picked[:count] + picked[count : 2 * count] + picked[2 * count : 3 * count]


def kernel(
    n_seg,
    n_band,
    scale,
    sft_hbm,
    doppler_hbm,
    antenna_hbm,
    index_hbm,
    offset_hbm,
    wing_hbm,
    out_ref,
    sft_ref,
    doppler_ref,
    antenna_ref,
    index_ref,
    offset_ref,
    wing_ref,
    param_ref,
    fine_ref,
    column_ref,
    x_ref,
    edge_ref,
    block_ref,
    load_sem,
    x_send,
    x_recv,
    edge_send,
    edge_recv,
    block_send,
    block_recv,
):
    seg = lax.axis_index("seg")
    band = lax.axis_index("band")
    segs_here, dets, _, bins = sft_ref.shape
    fine = index_ref.shape[1]
    own = fine // n_seg
    lines = 2 * dets
    has_up = band < n_band - 1
    has_down = band > 0
    up = jnp.minimum(band + 1, n_band - 1)
    down = jnp.maximum(band - 1, 0)
    peers = [lax.rem(seg + step, n_seg) for step in range(n_seg)]

    barrier = pltpu.get_barrier_semaphore()

    def greet(peer, there):
        pl.semaphore_signal(
            barrier, inc=1, device_id={"seg": peer, "band": there}, device_id_type=MESH
        )

    for peer in peers[1:]:
        greet(peer, band)
    for there, neighbour in ((has_up, up), (has_down, down)):

        @pl.when(there)
        def _():
            for peer in peers:
                greet(peer, neighbour)

    loads = []
    for source, target in (
        (sft_hbm, sft_ref),
        (doppler_hbm, doppler_ref),
        (antenna_hbm, antenna_ref),
        (index_hbm, index_ref),
        (offset_hbm, offset_ref),
        (wing_hbm, wing_ref),
    ):
        loads.append(pltpu.make_async_copy(source, target, load_sem.at[len(loads)]))
        loads[-1].start()
    loads[0].wait()
    for s in range(segs_here):
        for d in range(dets):
            first = s * lines + 2 * d
            x_ref[0, first : first + 2, :] = sft_ref[s, d].astype(jnp.float32)
    sides = has_up.astype(jnp.int32) + has_down.astype(jnp.int32)
    pl.semaphore_wait(barrier, n_seg - 1 + n_seg * sides)

    def edge_copy(side, step):
        start, neighbour = ((bins - LANES, up), (0, down))[side]
        return pltpu.make_async_remote_copy(
            src_ref=x_ref.at[0, :, pl.ds(start, LANES)],
            dst_ref=edge_ref.at[step, side],
            send_sem=edge_send.at[side, step],
            recv_sem=edge_recv.at[side, step],
            device_id={"seg": peers[step], "band": neighbour},
            device_id_type=MESH,
        )

    def x_copy(step):
        return pltpu.make_async_remote_copy(
            src_ref=x_ref.at[0],
            dst_ref=x_ref.at[step],
            send_sem=x_send.at[step - 1],
            recv_sem=x_recv.at[step - 1],
            device_id={"seg": peers[step], "band": band},
            device_id_type=MESH,
        )

    def block_copy(step):
        return pltpu.make_async_remote_copy(
            src_ref=column_ref.at[pl.ds(pl.multiple_of(peers[step] * own, own), own)],
            dst_ref=block_ref.at[step - 1],
            send_sem=block_send.at[step - 1],
            recv_sem=block_recv.at[step - 1],
            device_id={"seg": peers[step], "band": band},
            device_id_type=MESH,
        )

    for side, there in enumerate((has_up, has_down)):

        @pl.when(there)
        def _():
            for step in range(n_seg):
                edge_copy(side, step).start()

    for step in range(1, n_seg):
        x_copy(step).start()

    for load in loads[1:]:
        load.wait()
    param_ref[...] = jnp.zeros_like(param_ref)
    fine_ref[...] = jnp.zeros_like(fine_ref)
    for s in range(segs_here):
        param_ref[ROWS * s : ROWS * s + 1, :] = doppler_ref[s : s + 1, :]
        for q in range(2):
            first = ROWS * s + 1 + dets * q
            param_ref[first : first + dets, :] = antenna_ref[s, q]
    for s in range(segs_here):
        rows = gathered_rows(param_ref[ROWS * s : ROWS * (s + 1), :], index_ref[s : s + 1, :])
        fine_ref[ROWS * s : ROWS * (s + 1), :] = rows
        sine, cosine = half_turn(rows[0:1])
        fine_ref[ROWS * s + 5 : ROWS * s + 6, :] = offset_ref[s : s + 1, :].astype(jnp.float32)
        fine_ref[ROWS * s + 6 : ROWS * s + 7, :] = sine
        fine_ref[ROWS * s + 7 : ROWS * s + 8, :] = cosine
    column_ref[...] = jnp.transpose(fine_ref[...])
    for step in range(1, n_seg):
        block_copy(step).start()

    width = bins + 2 * (WMAX + OMAX)
    wing_low = jnp.where(has_down, wing_ref[down], 0)
    wing_mid = wing_ref[band]
    wing_high = jnp.where(has_up, wing_ref[up], 0)
    position = lax.broadcasted_iota(jnp.int32, (TAPS, width), 1)
    reach = jnp.where(
        position < OMAX, wing_low, jnp.where(position < OMAX + bins, wing_mid, wing_high)
    )
    tap_here = WMAX - 1 - lax.broadcasted_iota(jnp.int32, (TAPS, width), 0)
    inside = jnp.where((tap_here >= -reach) & (tap_here < reach), 1.0, 0.0).astype(jnp.bfloat16)

    lane = lax.broadcasted_iota(jnp.int32, (own, 2 * TAPS), 1)
    from_real = lane < TAPS
    tap = (WMAX - 1 - lax.rem(lane, TAPS)).astype(jnp.float32)

    def demodulators(columns, s):
        column = lambda row: columns[:, ROWS * s + row : ROWS * s + row + 1]
        u = tap - column(0)
        centre = u == 0.0
        envelope = jnp.where(
            centre, 1.0, -column(6) / jnp.where(centre, 1.0, math.pi * u)
        )
        real_part = envelope * column(7)
        imag_part = envelope * column(6)
        to_real = jnp.where(from_real, real_part, -imag_part)
        to_imag = jnp.where(from_real, imag_part, real_part)
        blocks = []
        for q in range(2):
            for shape in (to_real, to_imag):
                pieces = [column(1 + dets * q + d) * shape for d in range(dets)]
                blocks.append(jnp.concatenate(pieces, axis=1))
        return jnp.concatenate(blocks, axis=0).astype(jnp.bfloat16)

    total = jnp.zeros((own, bins), jnp.float32)
    for step in range(n_seg):
        if step == 0:
            columns = column_ref[pl.ds(pl.multiple_of(seg * own, own), own), :]
        else:
            block_copy(step).wait_recv()
            columns = block_ref[step - 1]
        kernels = [demodulators(columns, s) for s in range(segs_here)]
        for side, there in enumerate((has_down, has_up)):

            @pl.when(there)
            def _():
                edge_copy(side, step).wait_recv()

        if step > 0:
            x_copy(step).wait_recv()
        low = jnp.where(has_down, edge_ref[step, 0], 0.0)
        high = jnp.where(has_up, edge_ref[step, 1], 0.0)
        padded = jnp.concatenate([low, x_ref[step], high], axis=1)
        margin = LANES - WMAX - OMAX
        padded = pltpu.roll(padded, padded.shape[1] - margin, 1)[:, :width]
        for s in range(segs_here):
            unfolded = []
            for line in range(s * lines, (s + 1) * lines):
                spread = jnp.broadcast_to(padded[line : line + 1, :], (TAPS, width))
                spread = pltpu.roll(spread, width - TAPS + 1, 1, stride=1, stride_axis=0)
                unfolded.append(spread.astype(jnp.bfloat16) * inside)
            unfolded = jnp.concatenate(unfolded, axis=0)
            amplitude = jnp.dot(kernels[s], unfolded, preferred_element_type=jnp.float32)
            power = amplitude * amplitude
            coarse = (power[:own] + power[own : 2 * own]) + (
                power[2 * own : 3 * own] + power[3 * own :]
            )
            shift = columns[:, ROWS * s + 5 : ROWS * s + 6].astype(jnp.int32) + OMAX
            for bit in range((2 * OMAX).bit_length()):
                moved = pltpu.roll(coarse, width - (1 << bit), 1)
                coarse = jnp.where((shift & (1 << bit)) != 0, moved, coarse)
            total = total + coarse[:, :bins]
    out_ref[...] = total * scale

    for step in range(1, n_seg):
        x_copy(step).wait_send()
        block_copy(step).wait_send()
    for side, there in enumerate((has_up, has_down)):

        @pl.when(there)
        def _():
            for step in range(n_seg):
                edge_copy(side, step).wait_send()


def solution(mesh):
    n_seg = mesh.shape["seg"]
    n_band = mesh.shape["band"]
    placed = (
        P("seg", None, None, "band"),
        P("seg", None),
        P("seg", None, None, None),
        P("seg", None),
        P("seg", None),
        P(),
    )

    def per_device(sft, doppler, antenna, coarse_index, freq_offset, wing_width):
        segs_here, dets, _, bins = sft.shape
        fine = coarse_index.shape[1]
        own = fine // n_seg
        lines = segs_here * dets * 2
        operands = [
            pltpu.with_memory_space_constraint(operand, pltpu.HBM)
            for operand in (sft, doppler, antenna, coarse_index, freq_offset, wing_width)
        ]
        vmem = pl.BlockSpec(memory_space=pltpu.VMEM)
        hbm = pl.BlockSpec(memory_space=pltpu.HBM)
        return pl.pallas_call(
            functools.partial(kernel, n_seg, n_band, 0.25 / (segs_here * n_seg)),
            out_shape=jax.ShapeDtypeStruct((own, bins), jnp.float32),
            in_specs=[hbm] * 6,
            out_specs=vmem,
            scratch_shapes=[
                pltpu.VMEM(sft.shape, sft.dtype),
                pltpu.VMEM(doppler.shape, doppler.dtype),
                pltpu.VMEM(antenna.shape, antenna.dtype),
                pltpu.VMEM(coarse_index.shape, coarse_index.dtype),
                pltpu.VMEM(freq_offset.shape, freq_offset.dtype),
                pltpu.SMEM(wing_width.shape, wing_width.dtype),
                pltpu.VMEM((ROWS * segs_here, doppler.shape[1]), jnp.float32),
                pltpu.VMEM((LANES, fine), jnp.float32),
                pltpu.VMEM((fine, LANES), jnp.float32),
                pltpu.VMEM((n_seg, lines, bins), jnp.float32),
                pltpu.VMEM((n_seg, 2, lines, LANES), jnp.float32),
                pltpu.VMEM((n_seg - 1, own, LANES), jnp.float32),
                pltpu.SemaphoreType.DMA((6,)),
                pltpu.SemaphoreType.DMA((n_seg - 1,)),
                pltpu.SemaphoreType.DMA((n_seg - 1,)),
                pltpu.SemaphoreType.DMA((2, n_seg)),
                pltpu.SemaphoreType.DMA((2, n_seg)),
                pltpu.SemaphoreType.DMA((n_seg - 1,)),
                pltpu.SemaphoreType.DMA((n_seg - 1,)),
            ],
            compiler_params=pltpu.CompilerParams(
                collective_id=0, has_side_effects=True, vmem_limit_bytes=40 * 1024 * 1024
            ),
        )(*operands)

    return jax.shard_map(
        per_device, mesh=mesh, in_specs=placed, out_specs=P("seg", "band"), check_vma=False
    )
```

time: 12.2 us -> 12.4 us (1.016)
  the two profiles are of different devices: /device:TPU:1 before, /device:TPU:0 now
where the time goes in v1:
time: 12.4 us; the launch traced here: 12.3 us
  Pallas kernels  11.6 us (94%)
  local copies, waits for them, and re-layouts  0.62 us (5%)
    pallas_call x1, Pallas kernels, per_device(): pl.pallas_call(functools.partial(kernel, n_seg, n_band, 0.25 / (segs_here...  11.6 us
    unnamed x1, local copies, waits for them, and re-layouts  0.62 us

profile of v1, /device:TPU:0, one launch (start us, length us, event | category | flops | bytes accessed | tf_op | source)
XLA Modules:
  0.0 12.3 jit_solution(11364243570742348610)
XLA Ops:
  0.0 11.6 %shard_map.64 = f32[32,256]{1,0:T(8,128)S(1)} custom-call(bf16[2,2,2,256]{3,2,1,0:T(2,128)(2,1)} %sft_hbm.1, f32[2,512]{1,0:T(2,128)} %doppler_hbm.1, f32[2,2,2,512]{3,2,1,0:T(2,128)} %antenna_hbm.1, s32[2,128]{1,0:T(2,128)} %index_hbm.1, s32[2,128]{1,0:T(2,128)} %offset_hbm.1, s32[8]{0:T(128)} %wing_hbm.1), custom_call_target="tpu_custom_call" | custom-call | tf_op jit(solution)/shard_map/pallas_call | solution.py:291
  11.6 0.6 %copy.8 = f32[32,256]{1,0:T(8,128)} copy(f32[32,256]{1,0:T(8,128)S(1)} %shard_map.64) | data formatting | bytes 65536

commit v2 on v1

--- a/solution.py
+++ b/solution.py
@@ -10,7 +10,6 @@
 
 WMAX = 32
 OMAX = 32
-TAPS = 2 * WMAX
 LANES = 128
 ROWS = 8
 MESH = pl.DeviceIdType.MESH
@@ -181,23 +180,19 @@
     for step in range(1, n_seg):
         block_copy(step).start()
 
-    width = bins + 2 * (WMAX + OMAX)
-    wing_low = jnp.where(has_down, wing_ref[down], 0)
-    wing_mid = wing_ref[band]
-    wing_high = jnp.where(has_up, wing_ref[up], 0)
-    position = lax.broadcasted_iota(jnp.int32, (TAPS, width), 1)
-    reach = jnp.where(
-        position < OMAX, wing_low, jnp.where(position < OMAX + bins, wing_mid, wing_high)
-    )
-    tap_here = WMAX - 1 - lax.broadcasted_iota(jnp.int32, (TAPS, width), 0)
-    inside = jnp.where((tap_here >= -reach) & (tap_here < reach), 1.0, 0.0).astype(jnp.bfloat16)
-
-    lane = lax.broadcasted_iota(jnp.int32, (own, 2 * TAPS), 1)
-    from_real = lane < TAPS
-    tap = (WMAX - 1 - lax.rem(lane, TAPS)).astype(jnp.float32)
+    span = 2 * (WMAX + OMAX)
+    width = bins + span
+    wing_low = jnp.where(has_down, wing_ref[down], 0).astype(jnp.float32)
+    wing_mid = wing_ref[band].astype(jnp.float32)
+    wing_high = jnp.where(has_up, wing_ref[up], 0).astype(jnp.float32)
+    lane = lax.broadcasted_iota(jnp.int32, (own, span), 1)
+    reach = (span // 2 - 1 - lane).astype(jnp.float32)
+    place = lax.broadcasted_iota(jnp.int32, (own, bins), 1).astype(jnp.float32)
 
     def demodulators(columns, s):
         column = lambda row: columns[:, ROWS * s + row : ROWS * s + row + 1]
+        offset = column(5)
+        tap = reach - offset
         u = tap - column(0)
         centre = u == 0.0
         envelope = jnp.where(
@@ -205,53 +200,72 @@
         )
         real_part = envelope * column(7)
         imag_part = envelope * column(6)
-        to_real = jnp.where(from_real, real_part, -imag_part)
-        to_imag = jnp.where(from_real, imag_part, real_part)
         blocks = []
-        for q in range(2):
-            for shape in (to_real, to_imag):
-                pieces = [column(1 + dets * q + d) * shape for d in range(dets)]
-                blocks.append(jnp.concatenate(pieces, axis=1))
-        return jnp.concatenate(blocks, axis=0).astype(jnp.bfloat16)
-
-    total = jnp.zeros((own, bins), jnp.float32)
-    for step in range(n_seg):
-        if step == 0:
-            columns = column_ref[pl.ds(pl.multiple_of(seg * own, own), own), :]
-        else:
-            block_copy(step).wait_recv()
-            columns = block_ref[step - 1]
-        kernels = [demodulators(columns, s) for s in range(segs_here)]
+        for wing in (wing_mid, jnp.where(offset < 0.0, wing_low, wing_high)):
+            inside = (tap >= -wing) & (tap < wing)
+            real = jnp.where(inside, real_part, 0.0)
+            imag = jnp.where(inside, imag_part, 0.0)
+            for q in range(2):
+                to_real, to_imag = [], []
+                for d in range(dets):
+                    weight = column(1 + dets * q + d)
+                    weighted_real = (weight * real).astype(jnp.bfloat16)
+                    weighted_imag = (weight * imag).astype(jnp.bfloat16)
+                    to_real += [weighted_real, -weighted_imag]
+                    to_imag += [weighted_imag, weighted_real]
+                blocks.append(jnp.concatenate(to_real, axis=1))
+                blocks.append(jnp.concatenate(to_imag, axis=1))
+        return jnp.concatenate(blocks, axis=0)
+
+    def unfold(low, middle, high):
+        padded = jnp.concatenate(
+            [jnp.where(has_down, low, 0.0), middle, jnp.where(has_up, high, 0.0)], axis=1
+        )
+        margin = LANES - WMAX - OMAX
+        padded = pltpu.roll(padded, padded.shape[1] - margin, 1)[:, :width]
+        spreads = []
+        for line in range(segs_here * lines):
+            spread = jnp.broadcast_to(padded[line : line + 1, :], (span, width))
+            spread = pltpu.roll(spread, width - span + 1, 1, stride=1, stride_axis=0)
+            spreads.append(spread[:, :bins].astype(jnp.bfloat16))
+        return [
+            jnp.concatenate(spreads[s * lines : (s + 1) * lines], axis=0)
+            for s in range(segs_here)
+        ]
+
+    def moved_coarse(columns, s, kernels, unfolded):
+        amplitude = jnp.dot(kernels, unfolded, preferred_element_type=jnp.float32)
+        power = amplitude * amplitude
+        parts = [power[own * part : own * (part + 1)] for part in range(8)]
+        middle = (parts[0] + parts[1]) + (parts[2] + parts[3])
+        beside = (parts[4] + parts[5]) + (parts[6] + parts[7])
+        there = place + columns[:, ROWS * s + 5 : ROWS * s + 6]
+        return jnp.where((there >= 0.0) & (there < float(bins)), middle, beside)
+
+    def segment_sum(columns, x_slot):
+        unfolded = unfold(edge_ref[x_slot, 0], x_ref[x_slot], edge_ref[x_slot, 1])
+        result = None
+        for s in range(segs_here):
+            term = moved_coarse(columns, s, demodulators(columns, s), unfolded[s])
+            result = term if result is None else result + term
+        return result
+
+    def wait_edges(step):
         for side, there in enumerate((has_down, has_up)):
 
             @pl.when(there)
             def _():
                 edge_copy(side, step).wait_recv()
 
-        if step > 0:
-            x_copy(step).wait_recv()
-        low = jnp.where(has_down, edge_ref[step, 0], 0.0)
-        high = jnp.where(has_up, edge_ref[step, 1], 0.0)
-        padded = jnp.concatenate([low, x_ref[step], high], axis=1)
-        margin = LANES - WMAX - OMAX
-        padded = pltpu.roll(padded, padded.shape[1] - margin, 1)[:, :width]
-        for s in range(segs_here):
-            unfolded = []
-            for line in range(s * lines, (s + 1) * lines):
-                spread = jnp.broadcast_to(padded[line : line + 1, :], (TAPS, width))
-                spread = pltpu.roll(spread, width - TAPS + 1, 1, stride=1, stride_axis=0)
-                unfolded.append(spread.astype(jnp.bfloat16) * inside)
-            unfolded = jnp.concatenate(unfolded, axis=0)
-            amplitude = jnp.dot(kernels[s], unfolded, preferred_element_type=jnp.float32)
-            power = amplitude * amplitude
-            coarse = (power[:own] + power[own : 2 * own]) + (
-                power[2 * own : 3 * own] + power[3 * own :]
-            )
-            shift = columns[:, ROWS * s + 5 : ROWS * s + 6].astype(jnp.int32) + OMAX
-            for bit in range((2 * OMAX).bit_length()):
-                moved = pltpu.roll(coarse, width - (1 << bit), 1)
-                coarse = jnp.where((shift & (1 << bit)) != 0, moved, coarse)
-            total = total + coarse[:, :bins]
+    wait_edges(0)
+    columns = column_ref[pl.ds(pl.multiple_of(seg * own, own), own), :]
+    total = segment_sum(columns, 0)
+    for step in range(1, n_seg):
+        wait_edges(step)
+        x_copy(step).wait_recv()
+        block_copy(step).wait_recv()
+    for step in range(1, n_seg):
+        total = total + segment_sum(block_ref[step - 1], step)
     out_ref[...] = total * scale
 
     for step in range(1, n_seg):

time: 12.4 us -> 10.5 us (0.85)
  Pallas kernels: 11.6 us -> 9.66 us
    pallas_call x1, Pallas kernels: 11.6 us -> 9.66 us  [per_device(): pl.pallas_call(functools.partial(kernel, n_seg, n_band, 0.25 / (segs_here...]
where the time goes in v2:
time: 10.5 us; the launch traced here: 10.3 us
  Pallas kernels  9.66 us (92%)
  local copies, waits for them, and re-layouts  0.62 us (6%)
    pallas_call x1, Pallas kernels, per_device(): pl.pallas_call(functools.partial(kernel, n_seg, n_band, 0.25 / (segs_here...  9.66 us
    unnamed x1, local copies, waits for them, and re-layouts  0.62 us

profile of v2, /device:TPU:0, one launch (start us, length us, event | category | flops | bytes accessed | tf_op | source)
XLA Modules:
  0.0 10.3 jit_solution(11675837420163613825)
XLA Ops:
  0.0 9.7 %shard_map.64 = f32[32,256]{1,0:T(8,128)S(1)} custom-call(bf16[2,2,2,256]{3,2,1,0:T(2,128)(2,1)} %sft_hbm.1, f32[2,512]{1,0:T(2,128)} %doppler_hbm.1, f32[2,2,2,512]{3,2,1,0:T(2,128)} %antenna_hbm.1, s32[2,128]{1,0:T(2,128)} %index_hbm.1, s32[2,128]{1,0:T(2,128)} %offset_hbm.1, s32[8]{0:T(128)} %wing_hbm.1), custom_call_target="tpu_custom_call" | custom-call | tf_op jit(solution)/shard_map/pallas_call | solution.py:305
  9.7 0.6 %copy.8 = f32[32,256]{1,0:T(8,128)} copy(f32[32,256]{1,0:T(8,128)S(1)} %shard_map.64) | data formatting | bytes 65536

commit v3 on v2

--- a/solution.py
+++ b/solution.py
@@ -116,50 +116,6 @@
         for d in range(dets):
             first = s * lines + 2 * d
             x_ref[0, first : first + 2, :] = sft_ref[s, d].astype(jnp.float32)
-    sides = has_up.astype(jnp.int32) + has_down.astype(jnp.int32)
-    pl.semaphore_wait(barrier, n_seg - 1 + n_seg * sides)
-
-    def edge_copy(side, step):
-        start, neighbour = ((bins - LANES, up), (0, down))[side]
-        return pltpu.make_async_remote_copy(
-            src_ref=x_ref.at[0, :, pl.ds(start, LANES)],
-            dst_ref=edge_ref.at[step, side],
-            send_sem=edge_send.at[side, step],
-            recv_sem=edge_recv.at[side, step],
-            device_id={"seg": peers[step], "band": neighbour},
-            device_id_type=MESH,
-        )
-
-    def x_copy(step):
-        return pltpu.make_async_remote_copy(
-            src_ref=x_ref.at[0],
-            dst_ref=x_ref.at[step],
-            send_sem=x_send.at[step - 1],
-            recv_sem=x_recv.at[step - 1],
-            device_id={"seg": peers[step], "band": band},
-            device_id_type=MESH,
-        )
-
-    def block_copy(step):
-        return pltpu.make_async_remote_copy(
-            src_ref=column_ref.at[pl.ds(pl.multiple_of(peers[step] * own, own), own)],
-            dst_ref=block_ref.at[step - 1],
-            send_sem=block_send.at[step - 1],
-            recv_sem=block_recv.at[step - 1],
-            device_id={"seg": peers[step], "band": band},
-            device_id_type=MESH,
-        )
-
-    for side, there in enumerate((has_up, has_down)):
-
-        @pl.when(there)
-        def _():
-            for step in range(n_seg):
-                edge_copy(side, step).start()
-
-    for step in range(1, n_seg):
-        x_copy(step).start()
-
     for load in loads[1:]:
         load.wait()
     param_ref[...] = jnp.zeros_like(param_ref)
@@ -177,6 +133,50 @@
         fine_ref[ROWS * s + 6 : ROWS * s + 7, :] = sine
         fine_ref[ROWS * s + 7 : ROWS * s + 8, :] = cosine
     column_ref[...] = jnp.transpose(fine_ref[...])
+    sides = has_up.astype(jnp.int32) + has_down.astype(jnp.int32)
+    pl.semaphore_wait(barrier, n_seg - 1 + n_seg * sides)
+
+    def edge_copy(side, step):
+        start, neighbour = ((bins - LANES, up), (0, down))[side]
+        return pltpu.make_async_remote_copy(
+            src_ref=x_ref.at[0, :, pl.ds(start, LANES)],
+            dst_ref=edge_ref.at[step, side],
+            send_sem=edge_send.at[side, step],
+            recv_sem=edge_recv.at[side, step],
+            device_id={"seg": peers[step], "band": neighbour},
+            device_id_type=MESH,
+        )
+
+    def x_copy(step):
+        return pltpu.make_async_remote_copy(
+            src_ref=x_ref.at[0],
+            dst_ref=x_ref.at[step],
+            send_sem=x_send.at[step - 1],
+            recv_sem=x_recv.at[step - 1],
+            device_id={"seg": peers[step], "band": band},
+            device_id_type=MESH,
+        )
+
+    def block_copy(step):
+        return pltpu.make_async_remote_copy(
+            src_ref=column_ref.at[pl.ds(pl.multiple_of(peers[step] * own, own), own)],
+            dst_ref=block_ref.at[step - 1],
+            send_sem=block_send.at[step - 1],
+            recv_sem=block_recv.at[step - 1],
+            device_id={"seg": peers[step], "band": band},
+            device_id_type=MESH,
+        )
+
+    for side, there in enumerate((has_up, has_down)):
+
+        @pl.when(there)
+        def _():
+            for step in range(n_seg):
+                edge_copy(side, step).start()
+
+    for step in range(1, n_seg):
+        x_copy(step).start()
+
     for step in range(1, n_seg):
         block_copy(step).start()
 

time: 10.5 us -> 10.5 us (level)
  no operation moved by 1% of the time
where the time goes in v3:
time: 10.5 us; the launch traced here: 10.3 us
  Pallas kernels  9.67 us (92%)
  local copies, waits for them, and re-layouts  0.62 us (6%)
    pallas_call x1, Pallas kernels, per_device(): pl.pallas_call(functools.partial(kernel, n_seg, n_band, 0.25 / (segs_here...  9.67 us
    unnamed x1, local copies, waits for them, and re-layouts  0.62 us

profile of v3, /device:TPU:0, one launch (start us, length us, event | category | flops | bytes accessed | tf_op | source)
XLA Modules:
  0.0 10.3 jit_solution(17762111287647679807)
XLA Ops:
  0.0 9.7 %shard_map.64 = f32[32,256]{1,0:T(8,128)S(1)} custom-call(bf16[2,2,2,256]{3,2,1,0:T(2,128)(2,1)} %sft_hbm.1, f32[2,512]{1,0:T(2,128)} %doppler_hbm.1, f32[2,2,2,512]{3,2,1,0:T(2,128)} %antenna_hbm.1, s32[2,128]{1,0:T(2,128)} %index_hbm.1, s32[2,128]{1,0:T(2,128)} %offset_hbm.1, s32[8]{0:T(128)} %wing_hbm.1), custom_call_target="tpu_custom_call" | custom-call | tf_op jit(solution)/shard_map/pallas_call | solution.py:305
  9.7 0.6 %copy.8 = f32[32,256]{1,0:T(8,128)} copy(f32[32,256]{1,0:T(8,128)S(1)} %shard_map.64) | data formatting | bytes 65536

commit v4 on v3

--- a/solution.py
+++ b/solution.py
@@ -222,12 +222,17 @@
             [jnp.where(has_down, low, 0.0), middle, jnp.where(has_up, high, 0.0)], axis=1
         )
         margin = LANES - WMAX - OMAX
+        group = 2 * ROWS
         padded = pltpu.roll(padded, padded.shape[1] - margin, 1)[:, :width]
         spreads = []
         for line in range(segs_here * lines):
-            spread = jnp.broadcast_to(padded[line : line + 1, :], (span, width))
-            spread = pltpu.roll(spread, width - span + 1, 1, stride=1, stride_axis=0)
-            spreads.append(spread[:, :bins].astype(jnp.bfloat16))
+            rows = jnp.broadcast_to(padded[line : line + 1, :], (group, width))
+            rows = pltpu.roll(rows, 0, 1, stride=1, stride_axis=0).astype(jnp.bfloat16)
+            pieces = [
+                pltpu.roll(rows, width - span + 1 + first, 1)[:, :bins]
+                for first in range(0, span, group)
+            ]
+            spreads.append(jnp.concatenate(pieces, axis=0))
         return [
             jnp.concatenate(spreads[s * lines : (s + 1) * lines], axis=0)
             for s in range(segs_here)

time: 10.5 us -> 11.7 us (1.11)
  Pallas kernels: 9.67 us -> 10.9 us
    pallas_call x1, Pallas kernels: 9.67 us -> 10.9 us  [per_device(): pl.pallas_call(functools.partial(kernel, n_seg, n_band, 0.25 / (segs_here...]
where the time goes in v4:
time: 11.7 us; the launch traced here: 11.5 us
  Pallas kernels  10.9 us (93%)
  local copies, waits for them, and re-layouts  0.62 us (5%)
    pallas_call x1, Pallas kernels, per_device(): pl.pallas_call(functools.partial(kernel, n_seg, n_band, 0.25 / (segs_here...  10.9 us
    unnamed x1, local copies, waits for them, and re-layouts  0.62 us

profile of v4, /device:TPU:0, one launch (start us, length us, event | category | flops | bytes accessed | tf_op | source)
XLA Modules:
  0.0 11.5 jit_solution(11719985878020388110)
XLA Ops:
  0.0 10.9 %shard_map.64 = f32[32,256]{1,0:T(8,128)S(1)} custom-call(bf16[2,2,2,256]{3,2,1,0:T(2,128)(2,1)} %sft_hbm.1, f32[2,512]{1,0:T(2,128)} %doppler_hbm.1, f32[2,2,2,512]{3,2,1,0:T(2,128)} %antenna_hbm.1, s32[2,128]{1,0:T(2,128)} %index_hbm.1, s32[2,128]{1,0:T(2,128)} %offset_hbm.1, s32[8]{0:T(128)} %wing_hbm.1), custom_call_target="tpu_custom_call" | custom-call | tf_op jit(solution)/shard_map/pallas_call | solution.py:310
  10.9 0.6 %copy.8 = f32[32,256]{1,0:T(8,128)} copy(f32[32,256]{1,0:T(8,128)S(1)} %shard_map.64) | data formatting | bytes 65536

commit v5 on v0

--- a/solution.py
+++ b/solution.py
@@ -10,7 +10,6 @@
 
 WMAX = 32
 OMAX = 32
-TAPS = 2 * WMAX
 LANES = 128
 ROWS = 8
 MESH = pl.DeviceIdType.MESH
@@ -156,11 +155,19 @@
     columns = jnp.transpose(fine_ref[...])
     column_ref[...] = columns
 
-    lane = lax.broadcasted_iota(jnp.int32, (fine, 2 * TAPS), 1)
-    from_real = lane < TAPS
-    tap = (WMAX - 1 - lax.rem(lane, TAPS)).astype(jnp.float32)
-    for s in range(segs_here):
+    span = 2 * (WMAX + OMAX)
+    width = bins + span
+    wing_low = jnp.where(has_down, wing_ref[down], 0).astype(jnp.float32)
+    wing_mid = wing_ref[band].astype(jnp.float32)
+    wing_high = jnp.where(has_up, wing_ref[up], 0).astype(jnp.float32)
+    lane = lax.broadcasted_iota(jnp.int32, (fine, span), 1)
+    reach = (span // 2 - 1 - lane).astype(jnp.float32)
+    place = lax.broadcasted_iota(jnp.int32, (own, bins), 1).astype(jnp.float32)
+
+    def store_demodulators(columns, s):
         column = lambda row: columns[:, ROWS * s + row : ROWS * s + row + 1]
+        offset = column(5)
+        tap = reach - offset
         u = tap - column(0)
         centre = u == 0.0
         envelope = jnp.where(
@@ -168,26 +175,42 @@
         )
         real_part = envelope * column(7)
         imag_part = envelope * column(6)
-        to_real = jnp.where(from_real, real_part, -imag_part)
-        to_imag = jnp.where(from_real, imag_part, real_part)
-        for q in range(2):
-            for part, shape in enumerate((to_real, to_imag)):
+        blocks = []
+        for wing in (wing_mid, jnp.where(offset < 0.0, wing_low, wing_high)):
+            inside = (tap >= -wing) & (tap < wing)
+            real = jnp.where(inside, real_part, 0.0)
+            imag = jnp.where(inside, imag_part, 0.0)
+            for q in range(2):
+                to_real, to_imag = [], []
                 for d in range(dets):
-                    piece = column(1 + dets * q + d) * shape
-                    kernel_ref[s, 2 * q + part, :, 2 * TAPS * d : 2 * TAPS * (d + 1)] = (
-                        piece.astype(jnp.bfloat16)
-                    )
-
-    width = bins + 2 * (WMAX + OMAX)
-    wing_low = jnp.where(has_down, wing_ref[down], 0)
-    wing_mid = wing_ref[band]
-    wing_high = jnp.where(has_up, wing_ref[up], 0)
-    position = lax.broadcasted_iota(jnp.int32, (TAPS, width), 1)
-    reach = jnp.where(
-        position < OMAX, wing_low, jnp.where(position < OMAX + bins, wing_mid, wing_high)
-    )
-    tap_here = WMAX - 1 - lax.broadcasted_iota(jnp.int32, (TAPS, width), 0)
-    inside = (tap_here >= -reach) & (tap_here < reach)
+                    weight = column(1 + dets * q + d)
+                    weighted_real = (weight * real).astype(jnp.bfloat16)
+                    weighted_imag = (weight * imag).astype(jnp.bfloat16)
+                    to_real += [weighted_real, -weighted_imag]
+                    to_imag += [weighted_imag, weighted_real]
+                blocks.append(jnp.concatenate(to_real, axis=1))
+                blocks.append(jnp.concatenate(to_imag, axis=1))
+        for part, block in enumerate(blocks):
+            kernel_ref[s, part] = block
+
+    def unfold(low, middle, high):
+        padded = jnp.concatenate(
+            [jnp.where(has_down, low, 0.0), middle, jnp.where(has_up, high, 0.0)], axis=1
+        )
+        margin = LANES - WMAX - OMAX
+        padded = pltpu.roll(padded, padded.shape[1] - margin, 1)[:, :width]
+        spreads = []
+        for line in range(segs_here * lines):
+            spread = jnp.broadcast_to(padded[line : line + 1, :], (span, width))
+            spread = pltpu.roll(spread, width - span + 1, 1, stride=1, stride_axis=0)
+            spreads.append(spread[:, :bins].astype(jnp.bfloat16))
+        return [
+            jnp.concatenate(spreads[s * lines : (s + 1) * lines], axis=0)
+            for s in range(segs_here)
+        ]
+
+    for s in range(segs_here):
+        store_demodulators(columns, s)
 
     for side, there in enumerate((has_down, has_up)):
 
@@ -195,61 +218,55 @@
         def _():
             edge_copy(side).wait_recv()
 
-    low = jnp.where(has_down, edge_ref[0], 0.0)
-    high = jnp.where(has_up, edge_ref[1], 0.0)
-    padded = jnp.concatenate([low, x_ref[...], high], axis=1)
-    margin = LANES - WMAX - OMAX
-    padded = pltpu.roll(padded, padded.shape[1] - margin, 1)[:, :width]
-
-    transforms = []
-    for s in range(segs_here):
-        unfolded = []
-        for line in range(s * lines, (s + 1) * lines):
-            spread = jnp.broadcast_to(padded[line : line + 1, :], (TAPS, width))
-            spread = pltpu.roll(spread, width - TAPS + 1, 1, stride=1, stride_axis=0)
-            unfolded.append(jnp.where(inside, spread, 0.0))
-        transforms.append(jnp.concatenate(unfolded, axis=0).astype(jnp.bfloat16))
-
-    def fine_block(owner):
-        rows = pl.ds(pl.multiple_of(owner * own, own), own)
-        columns = column_ref[rows, :]
-        total = None
+    transforms = unfold(edge_ref[0], x_ref[...], edge_ref[1])
+
+    def fine_blocks(owners):
+        spans = [pl.ds(pl.multiple_of(owner * own, own), own) for owner in owners]
+        totals = [None] * len(owners)
         for s in range(segs_here):
-            taps = jnp.concatenate([kernel_ref[s, part, rows, :] for part in range(4)], axis=0)
-            amplitude = jnp.dot(taps, transforms[s], preferred_element_type=jnp.float32)
+            taps = [kernel_ref[s, part, rows, :] for rows in spans for part in range(8)]
+            amplitude = jnp.dot(
+                jnp.concatenate(taps, axis=0), transforms[s], preferred_element_type=jnp.float32
+            )
             power = amplitude * amplitude
-            coarse = (power[:own] + power[own : 2 * own]) + (
-                power[2 * own : 3 * own] + power[3 * own :]
-            )
-            shift = columns[:, ROWS * s + 5 : ROWS * s + 6].astype(jnp.int32) + OMAX
-            for bit in range((2 * OMAX).bit_length()):
-                moved = pltpu.roll(coarse, width - (1 << bit), 1)
-                coarse = jnp.where((shift & (1 << bit)) != 0, moved, coarse)
-            total = coarse[:, :bins] if total is None else total + coarse[:, :bins]
-        return total * scale
-
-    sends = []
+            for at, rows in enumerate(spans):
+                first = 8 * at
+                parts = [power[own * part : own * (part + 1)] for part in range(first, first + 8)]
+                middle = (parts[0] + parts[1]) + (parts[2] + parts[3])
+                beside = (parts[4] + parts[5]) + (parts[6] + parts[7])
+                there = place + column_ref[rows, ROWS * s + 5 : ROWS * s + 6]
+                moved = jnp.where((there >= 0.0) & (there < float(bins)), middle, beside)
+                totals[at] = moved if totals[at] is None else totals[at] + moved
+        return [total * scale for total in totals]
+
+    def part_copy(step):
+        return pltpu.make_async_remote_copy(
+            src_ref=part_ref.at[step - 1],
+            dst_ref=recv_ref.at[step - 1],
+            send_sem=part_send.at[step - 1],
+            recv_sem=part_recv.at[step - 1],
+            device_id={"seg": lax.rem(seg + step, n_seg)},
+            device_id_type=MESH,
+        )
+
+    half = (n_seg + 1) // 2
+    result = None
+    for steps in (list(range(half, n_seg)), list(range(1, half)) + [0]):
+        sums = fine_blocks([lax.rem(seg + step, n_seg) for step in steps])
+        for step, block in zip(steps, sums):
+            if step == 0:
+                result = block
+            else:
+                part_ref[step - 1] = block
+        for step in steps:
+            if step > 0:
+                part_copy(step).start()
     for step in range(1, n_seg):
-        peer = lax.rem(seg + step, n_seg)
-        part_ref[step - 1] = fine_block(peer)
-        sends.append(
-            pltpu.make_async_remote_copy(
-                src_ref=part_ref.at[step - 1],
-                dst_ref=recv_ref.at[step - 1],
-                send_sem=part_send.at[step - 1],
-                recv_sem=part_recv.at[step - 1],
-                device_id={"seg": peer},
-                device_id_type=MESH,
-            )
-        )
-        sends[-1].start()
-    result = fine_block(seg)
-    for step in range(1, n_seg):
-        sends[step - 1].wait_recv()
+        part_copy(step).wait_recv()
         result = result + recv_ref[step - 1]
     out_ref[...] = result
-    for send in sends:
-        send.wait_send()
+    for step in range(1, n_seg):
+        part_copy(step).wait_send()
     for side, there in enumerate((has_up, has_down)):
 
         @pl.when(there)
@@ -297,7 +314,7 @@
                 pltpu.VMEM((ROWS * segs_here, doppler.shape[1]), jnp.float32),
                 pltpu.VMEM((LANES, fine), jnp.float32),
                 pltpu.VMEM((fine, LANES), jnp.float32),
-                pltpu.VMEM((segs_here, 4, fine, 2 * TAPS * dets), jnp.bfloat16),
+                pltpu.VMEM((segs_here, 8, fine, 4 * (WMAX + OMAX) * dets), jnp.bfloat16),
                 pltpu.VMEM((n_seg - 1, own, bins), jnp.float32),
                 pltpu.VMEM((n_seg - 1, own, bins), jnp.float32),
                 pltpu.SemaphoreType.DMA((6,)),

time: 12.2 us -> 11.1 us (0.910)
  the two profiles are of different devices: /device:TPU:1 before, /device:TPU:0 now
where the time goes in v5:
time: 11.1 us; the launch traced here: 10.9 us
  Pallas kernels  10.3 us (93%)
  local copies, waits for them, and re-layouts  0.62 us (6%)
    pallas_call x1, Pallas kernels, per_device(): pl.pallas_call(functools.partial(kernel, n_seg, n_band, 0.25 / (segs_here...  10.3 us
    unnamed x1, local copies, waits for them, and re-layouts  0.62 us

profile of v5, /device:TPU:0, one launch (start us, length us, event | category | flops | bytes accessed | tf_op | source)
XLA Modules:
  0.0 10.9 jit_solution(1651148971572862091)
XLA Ops:
  0.0 10.3 %shard_map.64 = f32[32,256]{1,0:T(8,128)S(1)} custom-call(bf16[2,2,2,256]{3,2,1,0:T(2,128)(2,1)} %sft_hbm.1, f32[2,512]{1,0:T(2,128)} %doppler_hbm.1, f32[2,2,2,512]{3,2,1,0:T(2,128)} %antenna_hbm.1, s32[2,128]{1,0:T(2,128)} %index_hbm.1, s32[2,128]{1,0:T(2,128)} %offset_hbm.1, s32[8]{0:T(128)} %wing_hbm.1), custom_call_target="tpu_custom_call" | custom-call | tf_op jit(solution)/shard_map/pallas_call | solution.py:300
  10.3 0.6 %copy.8 = f32[32,256]{1,0:T(8,128)} copy(f32[32,256]{1,0:T(8,128)S(1)} %shard_map.64) | data formatting | bytes 65536

commit v6 on v2

--- a/solution.py
+++ b/solution.py
@@ -64,6 +64,7 @@
     x_ref,
     edge_ref,
     block_ref,
+    unfolded_ref,
     load_sem,
     x_send,
     x_recv,
@@ -242,14 +243,6 @@
         there = place + columns[:, ROWS * s + 5 : ROWS * s + 6]
         return jnp.where((there >= 0.0) & (there < float(bins)), middle, beside)
 
-    def segment_sum(columns, x_slot):
-        unfolded = unfold(edge_ref[x_slot, 0], x_ref[x_slot], edge_ref[x_slot, 1])
-        result = None
-        for s in range(segs_here):
-            term = moved_coarse(columns, s, demodulators(columns, s), unfolded[s])
-            result = term if result is None else result + term
-        return result
-
     def wait_edges(step):
         for side, there in enumerate((has_down, has_up)):
 
@@ -259,13 +252,25 @@
 
     wait_edges(0)
     columns = column_ref[pl.ds(pl.multiple_of(seg * own, own), own), :]
-    total = segment_sum(columns, 0)
+    unfolded = unfold(edge_ref[0, 0], x_ref[0], edge_ref[0, 1])
+    total = None
+    for s in range(segs_here):
+        term = moved_coarse(columns, s, demodulators(columns, s), unfolded[s])
+        total = term if total is None else total + term
     for step in range(1, n_seg):
         wait_edges(step)
         x_copy(step).wait_recv()
+    for step in range(1, n_seg):
+        unfolded = unfold(edge_ref[step, 0], x_ref[step], edge_ref[step, 1])
+        for s in range(segs_here):
+            unfolded_ref[step - 1, s] = unfolded[s]
+    for step in range(1, n_seg):
         block_copy(step).wait_recv()
     for step in range(1, n_seg):
-        total = total + segment_sum(block_ref[step - 1], step)
+        columns = block_ref[step - 1]
+        for s in range(segs_here):
+            kernels = demodulators(columns, s)
+            total = total + moved_coarse(columns, s, kernels, unfolded_ref[step - 1, s])
     out_ref[...] = total * scale
 
     for step in range(1, n_seg):
@@ -320,6 +325,9 @@
                 pltpu.VMEM((n_seg, lines, bins), jnp.float32),
                 pltpu.VMEM((n_seg, 2, lines, LANES), jnp.float32),
                 pltpu.VMEM((n_seg - 1, own, LANES), jnp.float32),
+                pltpu.VMEM(
+                    (n_seg - 1, segs_here, 4 * (WMAX + OMAX) * dets, bins), jnp.bfloat16
+                ),
                 pltpu.SemaphoreType.DMA((6,)),
                 pltpu.SemaphoreType.DMA((n_seg - 1,)),
                 pltpu.SemaphoreType.DMA((n_seg - 1,)),

time: 10.5 us -> 10.5 us (level)
  no operation moved by 1% of the time
where the time goes in v6:
time: 10.5 us; the launch traced here: 10.3 us
  Pallas kernels  9.69 us (92%)
  local copies, waits for them, and re-layouts  0.62 us (6%)
    pallas_call x1, Pallas kernels, per_device(): pl.pallas_call(functools.partial(kernel, n_seg, n_band, 0.25 / (segs_here...  9.69 us
    unnamed x1, local copies, waits for them, and re-layouts  0.62 us

profile of v6, /device:TPU:0, one launch (start us, length us, event | category | flops | bytes accessed | tf_op | source)
XLA Modules:
  0.0 10.3 jit_solution(12636521184238453614)
XLA Ops:
  0.0 9.7 %shard_map.64 = f32[32,256]{1,0:T(8,128)S(1)} custom-call(bf16[2,2,2,256]{3,2,1,0:T(2,128)(2,1)} %sft_hbm.1, f32[2,512]{1,0:T(2,128)} %doppler_hbm.1, f32[2,2,2,512]{3,2,1,0:T(2,128)} %antenna_hbm.1, s32[2,128]{1,0:T(2,128)} %index_hbm.1, s32[2,128]{1,0:T(2,128)} %offset_hbm.1, s32[8]{0:T(128)} %wing_hbm.1), custom_call_target="tpu_custom_call" | custom-call | tf_op jit(solution)/shard_map/pallas_call | solution.py:310
  9.7 0.6 %copy.8 = f32[32,256]{1,0:T(8,128)} copy(f32[32,256]{1,0:T(8,128)S(1)} %shard_map.64) | data formatting | bytes 65536

commit v7 on v3

--- a/solution.py
+++ b/solution.py
@@ -222,12 +222,23 @@
             [jnp.where(has_down, low, 0.0), middle, jnp.where(has_up, high, 0.0)], axis=1
         )
         margin = LANES - WMAX - OMAX
+        tile_lane = lax.broadcasted_iota(jnp.int32, (ROWS, LANES), 1)
         padded = pltpu.roll(padded, padded.shape[1] - margin, 1)[:, :width]
         spreads = []
         for line in range(segs_here * lines):
-            spread = jnp.broadcast_to(padded[line : line + 1, :], (span, width))
-            spread = pltpu.roll(spread, width - span + 1, 1, stride=1, stride_axis=0)
-            spreads.append(spread[:, :bins].astype(jnp.bfloat16))
+            rows = jnp.broadcast_to(padded[line : line + 1, :], (ROWS, width))
+            rows = pltpu.roll(rows, 0, 1, stride=1, stride_axis=0)
+            tiles = [rows[:, at : at + LANES] for at in range(0, width, LANES)]
+            pieces = []
+            for first in range(0, span, ROWS):
+                back = LANES - (span - 1 - first)
+                turned = [pltpu.roll(tile, back, 1) for tile in tiles]
+                chosen = [
+                    jnp.where(tile_lane < back, turned[at], turned[at + 1])
+                    for at in range(bins // LANES)
+                ]
+                pieces.append(jnp.concatenate(chosen, axis=1))
+            spreads.append(jnp.concatenate(pieces, axis=0).astype(jnp.bfloat16))
         return [
             jnp.concatenate(spreads[s * lines : (s + 1) * lines], axis=0)
             for s in range(segs_here)

time: 10.5 us -> 12.3 us (1.17)
  Pallas kernels: 9.67 us -> 11.5 us
    pallas_call x1, Pallas kernels: 9.67 us -> 11.5 us  [per_device(): pl.pallas_call(functools.partial(kernel, n_seg, n_band, 0.25 / (segs_here...]
where the time goes in v7:
time: 12.3 us; the launch traced here: 12.1 us
  Pallas kernels  11.5 us (93%)
  local copies, waits for them, and re-layouts  0.62 us (5%)
    pallas_call x1, Pallas kernels, per_device(): pl.pallas_call(functools.partial(kernel, n_seg, n_band, 0.25 / (segs_here...  11.5 us
    unnamed x1, local copies, waits for them, and re-layouts  0.62 us

profile of v7, /device:TPU:0, one launch (start us, length us, event | category | flops | bytes accessed | tf_op | source)
XLA Modules:
  0.0 12.1 jit_solution(5130167456559517535)
XLA Ops:
  0.0 11.5 %shard_map.64 = f32[32,256]{1,0:T(8,128)S(1)} custom-call(bf16[2,2,2,256]{3,2,1,0:T(2,128)(2,1)} %sft_hbm.1, f32[2,512]{1,0:T(2,128)} %doppler_hbm.1, f32[2,2,2,512]{3,2,1,0:T(2,128)} %antenna_hbm.1, s32[2,128]{1,0:T(2,128)} %index_hbm.1, s32[2,128]{1,0:T(2,128)} %offset_hbm.1, s32[8]{0:T(128)} %wing_hbm.1), custom_call_target="tpu_custom_call" | custom-call | tf_op jit(solution)/shard_map/pallas_call | solution.py:316
  11.5 0.6 %copy.8 = f32[32,256]{1,0:T(8,128)} copy(f32[32,256]{1,0:T(8,128)S(1)} %shard_map.64) | data formatting | bytes 65536

commit v8 on v3

--- a/solution.py
+++ b/solution.py
@@ -222,12 +222,20 @@
             [jnp.where(has_down, low, 0.0), middle, jnp.where(has_up, high, 0.0)], axis=1
         )
         margin = LANES - WMAX - OMAX
+        row_at = lax.broadcasted_iota(jnp.int32, (span, LANES), 0)
+        this_tile = lax.broadcasted_iota(jnp.int32, (span, LANES), 1) <= row_at
         padded = pltpu.roll(padded, padded.shape[1] - margin, 1)[:, :width]
         spreads = []
         for line in range(segs_here * lines):
-            spread = jnp.broadcast_to(padded[line : line + 1, :], (span, width))
-            spread = pltpu.roll(spread, width - span + 1, 1, stride=1, stride_axis=0)
-            spreads.append(spread[:, :bins].astype(jnp.bfloat16))
+            turned = []
+            for at in range(0, width, LANES):
+                tile = jnp.broadcast_to(padded[line : line + 1, at : at + LANES], (span, LANES))
+                turned.append(pltpu.roll(tile, LANES + 1 - span, 1, stride=1, stride_axis=0))
+            chosen = [
+                jnp.where(this_tile, turned[at], turned[at + 1]).astype(jnp.bfloat16)
+                for at in range(bins // LANES)
+            ]
+            spreads.append(jnp.concatenate(chosen, axis=1))
         return [
             jnp.concatenate(spreads[s * lines : (s + 1) * lines], axis=0)
             for s in range(segs_here)

time: 10.5 us -> 10.5 us (level)
  no operation moved by 1% of the time
where the time goes in v8:
time: 10.5 us; the launch traced here: 10.3 us
  Pallas kernels  9.67 us (92%)
  local copies, waits for them, and re-layouts  0.62 us (6%)
    pallas_call x1, Pallas kernels, per_device(): pl.pallas_call(functools.partial(kernel, n_seg, n_band, 0.25 / (segs_here...  9.67 us
    unnamed x1, local copies, waits for them, and re-layouts  0.62 us

profile of v8, /device:TPU:0, one launch (start us, length us, event | category | flops | bytes accessed | tf_op | source)
XLA Modules:
  0.0 10.3 jit_solution(14305431114426102159)
XLA Ops:
  0.0 9.7 %shard_map.64 = f32[32,256]{1,0:T(8,128)S(1)} custom-call(bf16[2,2,2,256]{3,2,1,0:T(2,128)(2,1)} %sft_hbm.1, f32[2,512]{1,0:T(2,128)} %doppler_hbm.1, f32[2,2,2,512]{3,2,1,0:T(2,128)} %antenna_hbm.1, s32[2,128]{1,0:T(2,128)} %index_hbm.1, s32[2,128]{1,0:T(2,128)} %offset_hbm.1, s32[8]{0:T(128)} %wing_hbm.1), custom_call_target="tpu_custom_call" | custom-call | tf_op jit(solution)/shard_map/pallas_call | solution.py:313
  9.7 0.6 %copy.8 = f32[32,256]{1,0:T(8,128)} copy(f32[32,256]{1,0:T(8,128)S(1)} %shard_map.64) | data formatting | bytes 65536

commit v9 on v8

--- a/solution.py
+++ b/solution.py
@@ -250,11 +250,11 @@
         there = place + columns[:, ROWS * s + 5 : ROWS * s + 6]
         return jnp.where((there >= 0.0) & (there < float(bins)), middle, beside)
 
-    def segment_sum(columns, x_slot):
+    def segment_sum(columns, kernels, x_slot):
         unfolded = unfold(edge_ref[x_slot, 0], x_ref[x_slot], edge_ref[x_slot, 1])
         result = None
         for s in range(segs_here):
-            term = moved_coarse(columns, s, demodulators(columns, s), unfolded[s])
+            term = moved_coarse(columns, s, kernels[s], unfolded[s])
             result = term if result is None else result + term
         return result
 
@@ -265,15 +265,18 @@
             def _():
                 edge_copy(side, step).wait_recv()
 
+    columns = column_ref[pl.ds(pl.multiple_of(seg * own, own), own), :]
+    kernels = [demodulators(columns, s) for s in range(segs_here)]
     wait_edges(0)
-    columns = column_ref[pl.ds(pl.multiple_of(seg * own, own), own), :]
-    total = segment_sum(columns, 0)
+    total = segment_sum(columns, kernels, 0)
     for step in range(1, n_seg):
         wait_edges(step)
         x_copy(step).wait_recv()
         block_copy(step).wait_recv()
     for step in range(1, n_seg):
-        total = total + segment_sum(block_ref[step - 1], step)
+        columns = block_ref[step - 1]
+        kernels = [demodulators(columns, s) for s in range(segs_here)]
+        total = total + segment_sum(columns, kernels, step)
     out_ref[...] = total * scale
 
     for step in range(1, n_seg):

time: 10.5 us -> 10.3 us (0.981)
  Pallas kernels: 9.67 us -> 9.52 us
    pallas_call x1, Pallas kernels: 9.67 us -> 9.52 us  [per_device(): pl.pallas_call(functools.partial(kernel, n_seg, n_band, 0.25 / (segs_here...]
where the time goes in v9:
time: 10.3 us; the launch traced here: 10.1 us
  Pallas kernels  9.52 us (92%)
  local copies, waits for them, and re-layouts  0.62 us (6%)
    pallas_call x1, Pallas kernels, per_device(): pl.pallas_call(functools.partial(kernel, n_seg, n_band, 0.25 / (segs_here...  9.52 us
    unnamed x1, local copies, waits for them, and re-layouts  0.62 us

profile of v9, /device:TPU:0, one launch (start us, length us, event | category | flops | bytes accessed | tf_op | source)
XLA Modules:
  0.0 10.1 jit_solution(16649733210213228343)
XLA Ops:
  0.0 9.5 %shard_map.64 = f32[32,256]{1,0:T(8,128)S(1)} custom-call(bf16[2,2,2,256]{3,2,1,0:T(2,128)(2,1)} %sft_hbm.1, f32[2,512]{1,0:T(2,128)} %doppler_hbm.1, f32[2,2,2,512]{3,2,1,0:T(2,128)} %antenna_hbm.1, s32[2,128]{1,0:T(2,128)} %index_hbm.1, s32[2,128]{1,0:T(2,128)} %offset_hbm.1, s32[8]{0:T(128)} %wing_hbm.1), custom_call_target="tpu_custom_call" | custom-call | tf_op jit(solution)/shard_map/pallas_call | solution.py:316
  9.5 0.6 %copy.8 = f32[32,256]{1,0:T(8,128)} copy(f32[32,256]{1,0:T(8,128)S(1)} %shard_map.64) | data formatting | bytes 65536
